TPU v7x, 32 devices: a whole 2x2x4 slice. The times are simulated.
32 devices in a mesh: groups: 2 (over x), ctx: 16 (over z, y, core).
Axes of the slice: x: 2, y: 2, z: 4, core: 2. Of those that a mesh axis runs over, the one named last changes fastest.
Arguments:
- tokens: bfloat16 [16384, 2048], P(('groups', 'ctx')), parts along dimension 0, may hold values from -14 to 14, as said below
- projected: bfloat16 [16384, 6144], P(('groups', 'ctx')), parts along dimension 0, may hold values from -6 to 6
- short_filter: float32 [3, 6144], replicated, may hold values from -3 to 3
- long_filter: bfloat16 [128, 128], replicated, may hold values from -0.5 to 0.5
- conv_bias: float32 [2048], replicated, may hold values from 0.5 to 1.5
- out_weight: bfloat16 [2048, 2048], P(None, 'ctx'), may hold values from -0.125 to 0.125
Outputs:
- result: bfloat16 [16384, 2048], P(('groups', 'ctx')), parts along dimension 0
There are 2 independent parts, one for each index of `groups`. A program takes and returns all parts, laid end to end along the dimension named above; an argument that names none is the same for every part. Nothing has to cross between parts.
Inputs may be any that keep to these rules, and one draw needn't show every extreme that they name: `tokens`: activations of the residual stream.
All inputs are finite; a program needn't handle non-finite values.
Results may differ from a plain program's by a relative error of at most 0.012.
Values may be sent and summed in bfloat16 or wider, within the bound.
A program may use at most 128 MiB of HBM per device.

v0:
```python
import jax
import jax.numpy as jnp
from jax import lax
from jax.sharding import PartitionSpec as P


def shifted(block, axis, distance):
    devices = range(lax.axis_size(axis))
    route = [(i - distance, i) for i in devices if i - distance in devices]
    return lax.ppermute(block, axis, route)


def short_mixed(padded, short_filter, row_count):
    source = padded.astype(jnp.float32)
    total = short_filter[0] * source[2 : 2 + row_count]
    total = total + short_filter[1] * source[1 : 1 + row_count]
    return total + short_filter[2] * source[0:row_count]


def split_gates(mixed, channels):
    gate_rows = mixed[:, :channels]
    carried = (mixed[:, channels : 2 * channels] * mixed[:, 2 * channels :]).astype(jnp.bfloat16)
    return (gate_rows, carried)


def long_conv(extended, long_filter, row_count):
    filters, tap_count = long_filter.shape
    block = min(128, row_count)
    span = block + tap_count - 1
    reversed_taps = long_filter[:, ::-1]
    pattern = jnp.concatenate(
        [reversed_taps, jnp.zeros((filters, block), long_filter.dtype)], axis=1
    )
    toeplitz = jnp.tile(pattern, (1, block))[:, : block * span].reshape(filters, block, span)
    grouped = extended.reshape(extended.shape[0], filters, -1)

    def one_block(index):
        window = lax.dynamic_slice_in_dim(grouped, index * block, span, 0)
        part_conv = jnp.einsum("gts,sgc->tgc", toeplitz, window, preferred_element_type=jnp.float32)
        return part_conv.reshape(block, -1)

    blocks = lax.map(one_block, jnp.arange(row_count // block, dtype=jnp.int32))
    return blocks.reshape(row_count, -1)


def on_device(tokens, projected, short_filter, long_filter, conv_bias, out_weight):
    row_count = tokens.shape[0]
    tap_count = long_filter.shape[1]
    channels = out_weight.shape[0]
    edge_rows = shifted(projected[row_count - 2 :], "ctx", 1)
    mixed = short_mixed(jnp.concatenate([edge_rows, projected], axis=0), short_filter, row_count)
    gate_rows, carried = split_gates(mixed, channels)
    carried_edge = shifted(carried[row_count - tap_count + 1 :], "ctx", 1)
    extended = jnp.concatenate([carried_edge, carried], axis=0)
    conv = long_conv(extended, long_filter, row_count)
    gated = (gate_rows * (conv + conv_bias * carried.astype(jnp.float32))).astype(jnp.bfloat16)
    branch = jnp.dot(
        gated,
        lax.all_gather(out_weight, "ctx", axis=1, tiled=True),
        preferred_element_type=jnp.float32,
    )
    return (tokens.astype(jnp.float32) + branch).astype(jnp.bfloat16)


def solution(mesh):
    placed = (P(("groups", "ctx"), None), P(("groups", "ctx"), None), P(), P(), P(), P(None, "ctx"))
    return jax.shard_map(
        on_device, mesh=mesh, in_specs=placed, out_specs=P(("groups", "ctx"), None), check_vma=False
    )
```

profile of v0, /device:TPU:1, one launch (start us, length us, event | category | flops | bytes accessed | tf_op | source)
XLA Modules:
  0.0 152.6 jit_solution(11511301803925277580)
XLA Ops:
  7.3 0.9 slice.37
  8.2 4.5 %collective-permute-start = (bf16[2,6144]{1,0:T(2,128)(2,1)S(1)}, bf16[2,6144]{1,0:T(2,128)(2,1)S(1)}, u32[]{:S(2)}, u32[]{:S(2)}) collective-permute-start(bf16[2,6144]{1,0:T(2,128)(2,1)S(1)} %slice.37), channel_id=1, source_target_pairs={{0,1},{1,2},{2,3},{3,4},{4,5},{5,6},{6,7},{7,8},{8,9},{9,10},{10,1... | collective-permute-start | bytes 73736 | tf_op jit(solution)/shard_map/ppermute | solution.py:10
  12.7 1.1 fusion.7
  13.9 4.7 %maximum_convert_fusion = f32[514,6144]{1,0:T(8,128)S(1)} fusion(bf16[512,6144]{1,0:T(8,128)(2,1)} %param.9, bf16[2,6144]{1,0:T(2,128)(2,1)S(1)} %collective-permute-done), kind=kLoop, calls=%fused_computation.9 | loop fusion | flops 12632064 | bytes 18948096 | tf_op jit(solution)/shard_map/convert_element_type | solution.py:14
  18.5 6.6 %fusion.3 = f32[512,6144]{1,0:T(8,128)} fusion(f32[514,6144]{1,0:T(8,128)S(1)} %maximum_convert_fusion, f32[6144]{0:T(1024)S(1)} %bitcast.28, f32[6144]{0:T(1024)S(1)} %bitcast.29, f32[6144]{0:T(1024)S(1)} %bitcast.27), kind=kLoop, calls=%fused_computation.5 | loop fusion | flops 15728640 | bytes 50405376 | tf_op jit(solution)/shard_map/add | solution.py:17
  25.1 4.1 %fusion.5 = bf16[512,2048]{1,0:T(8,128)(2,1)S(1)} fusion(f32[512,6144]{1,0:T(8,128)} %fusion.3), kind=kLoop, calls=%fused_computation.11 | loop fusion | flops 2097152 | bytes 10485760 | tf_op jit(solution)/shard_map/convert_element_type | solution.py:22
  29.4 4.0 %collective-permute-start.1 = (bf16[127,2048]{1,0:T(8,128)(2,1)S(1)}, bf16[127,2048]{1,0:T(8,128)(2,1)S(1)}, u32[]{:S(2)}, u32[]{:S(2)}) collective-permute-start(bf16[127,2048]{1,0:T(8,128)(2,1)S(1)} %slice.54), channel_id=1, source_target_pairs={{0,1},{1,2},{2,3},{3,4},{4,5},{5,6},{6,7},{7,8},{8,9},{9,10},{10,1... | collective-permute-start | bytes 1560584 | tf_op jit(solution)/shard_map/ppermute | solution.py:10
  33.5 3.9 %tile.4 = bf16[128,128,256]{2,1,0:T(8,128)(2,1)} broadcast(bf16[128,256]{1,0:T(8,128)(2,1)S(1)} %concatenate.11), dimensions={0,2} | broadcast | bytes 8454144 | tf_op jit(solution)/shard_map/tile | solution.py:34
  37.5 12.7 %copy.14 = bf16[16,8,128,256]{3,1,2,0:T(8,128)(2,1)} copy(bf16[16,8,128,256]{3,2,1,0:T(8,128)(2,1)} %bitcast.24) | data formatting | bytes 16777216
  50.2 7.4 %slice.55 = bf16[128,32640]{1,0:T(8,128)(2,1)} slice(bf16[128,32768]{1,0:T(8,128)(2,1)} %bitcast.25), slice={[0:128], [0:32640]} | slice | bytes 16711680 | tf_op jit(solution)/shard_map/slice | solution.py:34
  57.6 29.6 %reshape.19 = bf16[128,128,255]{2,1,0:T(8,128)(2,1)} reshape(bf16[128,32640]{1,0:T(8,128)(2,1)} %slice.55) | data formatting | bytes 16711680 | tf_op jit(solution)/shard_map/reshape | solution.py:34
  87.2 2.0 %pad_maximum_fusion = bf16[639,2048]{1,0:T(8,128)(2,1)} fusion(bf16[512,2048]{1,0:T(8,128)(2,1)S(1)} %fusion.5, bf16[127,2048]{1,0:T(8,128)(2,1)S(1)} %collective-permute-done.1), kind=kLoop, calls=%fused_computation.16 | loop fusion | flops 5234688 | bytes 5234688 | tf_op jit(solution)/shard_map/concatenate | solution.py:54
  89.2 4.5 %copy.10 = bf16[639,2048]{0,1:T(8,128)(2,1)} copy(bf16[639,2048]{1,0:T(8,128)(2,1)} %pad_maximum_fusion) | data formatting | bytes 5234688 | tf_op jit(solution)/shard_map/concatenate | solution.py:54
  93.7 34.9 %while.10 = (s32[]{:T(128)}, f32[4,128,2048]{2,1,0:T(8,128)}, s32[4]{0:T(128)S(1)}, bf16[639,128,16]{0,2,1:T(8,128)(2,1)}, bf16[128,128,255]{2,1,0:T(8,128)(2,1)...) while((s32[]{:T(128)}, f32[4,128,2048]{2,1,0:T(8,128)}, s32[4]{0:T(128)S(1)}, ...), condition=%wide.region_1.2_spmd, body=%wide.region_0.1_spmd.sunk | while | flops 133693448 | bytes 14680731 | solution.py:42
  94.8 6.2 %fusion.16 = f32[128,16,128]{2,1,0:T(8,128)S(1)} fusion(bf16[128,128,255]{2,1,0:T(8,128)(2,1)} %get-tuple-element.104, bf16[639,128,16]{0,2,1:T(8,128)(2,1)} %get-tuple-element.103, s32[]{:T(128)S(6)} %select_n.4), kind=kOutput, calls=%fused_computation.clone.1 | convolution fusion | flops 133693440 | bytes 10485764 | tf_op jit(solution)/shard_map/while/body/eval_jaxpr/gts,sgc->tgc/dot_general | solution.py:39
  101.4 1.1 constant_dynamic-update-slice_fusion.2
  103.6 6.2 %fusion.16 = f32[128,16,128]{2,1,0:T(8,128)S(1)} fusion(bf16[128,128,255]{2,1,0:T(8,128)(2,1)} %get-tuple-element.104, bf16[639,128,16]{0,2,1:T(8,128)(2,1)} %get-tuple-element.103, s32[]{:T(128)S(6)} %select_n.4), kind=kOutput, calls=%fused_computation.clone.1 | convolution fusion | flops 133693440 | bytes 10485764 | tf_op jit(solution)/shard_map/while/body/eval_jaxpr/gts,sgc->tgc/dot_general | solution.py:39
  110.1 1.0 constant_dynamic-update-slice_fusion.2
  112.3 6.2 %fusion.16 = f32[128,16,128]{2,1,0:T(8,128)S(1)} fusion(bf16[128,128,255]{2,1,0:T(8,128)(2,1)} %get-tuple-element.104, bf16[639,128,16]{0,2,1:T(8,128)(2,1)} %get-tuple-element.103, s32[]{:T(128)S(6)} %select_n.4), kind=kOutput, calls=%fused_computation.clone.1 | convolution fusion | flops 133693440 | bytes 10485764 | tf_op jit(solution)/shard_map/while/body/eval_jaxpr/gts,sgc->tgc/dot_general | solution.py:39
  118.8 1.1 constant_dynamic-update-slice_fusion.2
  121.1 6.0 %fusion.16 = f32[128,16,128]{2,1,0:T(8,128)S(1)} fusion(bf16[128,128,255]{2,1,0:T(8,128)(2,1)} %get-tuple-element.104, bf16[639,128,16]{0,2,1:T(8,128)(2,1)} %get-tuple-element.103, s32[]{:T(128)S(6)} %select_n.4), kind=kOutput, calls=%fused_computation.clone.1 | convolution fusion | flops 133693440 | bytes 10485764 | tf_op jit(solution)/shard_map/while/body/eval_jaxpr/gts,sgc->tgc/dot_general | solution.py:39
  127.5 1.1 constant_dynamic-update-slice_fusion.2
  128.5 7.8 %fusion.6 = bf16[512,2048]{1,0:T(8,128)(2,1)S(1)} fusion(f32[512,6144]{1,0:T(8,128)} %fusion.3, f32[4,128,2048]{2,1,0:T(8,128)} %get-tuple-element.32, f32[2048]{0:T(1024)S(1)} %copy-done.1), kind=kLoop, calls=%fused_computation.13 | loop fusion | flops 7340032 | bytes 18882560 | tf_op jit(solution)/shard_map/convert_element_type | solution.py:56
  136.4 9.4 %add_convert_fusion = bf16[512,2048]{1,0:T(8,128)(2,1)} fusion(bf16[512,2048]{1,0:T(8,128)(2,1)} %param.8, bf16[512,2048]{1,0:T(8,128)(2,1)S(1)} %fusion.6, bf16[2048,2048]{1,0:T(8,128)(2,1)} %all-gather.2.cloned.1.call-done), kind=kOutput, calls=%fused_computation.15 | convolution fusion | flops 4298113024 | bytes 14680064 | tf_op jit(solution)/shard_map/dot_general | solution.py:57
  (22 shorter events, 4.7 us)
Async XLA Ops:
  6.5 129.8 %all-gather.2.cloned.1.call-start = ((), (), s32[]{:S(2)}) async-start(), calls=%async_computation | async-start | bytes 8912896 | tf_op jit(solution)/shard_map/all_gather | solution.py:59
  8.2 5.7 %collective-permute-start = (bf16[2,6144]{1,0:T(2,128)(2,1)S(1)}, bf16[2,6144]{1,0:T(2,128)(2,1)S(1)}, u32[]{:S(2)}, u32[]{:S(2)}) collective-permute-start(bf16[2,6144]{1,0:T(2,128)(2,1)S(1)} %slice.37), channel_id=1, source_target_pairs={{0,1},{1,2},{2,3},{3,4},{4,5},{5,6},{6,7},{7,8},{8,9},{9,10},{10,1... | collective-permute-start | bytes 73736 | tf_op jit(solution)/shard_map/ppermute | solution.py:10
  25.1 8.3 %copy-start = (bf16[128,128]{1,0:T(8,128)(2,1)S(1)}, bf16[128,128]{1,0:T(8,128)(2,1)}, u32[]{:S(2)}) copy-start(bf16[128,128]{1,0:T(8,128)(2,1)} %param.11) | copy-start | bytes 98308
  29.4 57.8 %collective-permute-start.1 = (bf16[127,2048]{1,0:T(8,128)(2,1)S(1)}, bf16[127,2048]{1,0:T(8,128)(2,1)S(1)}, u32[]{:S(2)}, u32[]{:S(2)}) collective-permute-start(bf16[127,2048]{1,0:T(8,128)(2,1)S(1)} %slice.54), channel_id=1, source_target_pairs={{0,1},{1,2},{2,3},{3,4},{4,5},{5,6},{6,7},{7,8},{8,9},{9,10},{10,1... | collective-permute-start | bytes 1560584 | tf_op jit(solution)/shard_map/ppermute | solution.py:10
  93.7 34.9 %copy-start.1 = (f32[2048]{0:T(1024)S(1)}, f32[2048]{0:T(1024)}, u32[]{:S(2)}) copy-start(f32[2048]{0:T(1024)} %param.12) | copy-start | bytes 24580
Sparse Core Ops, SparseCore 0:
  9.5 82.1 all-gather.1
where the time goes:
time: 153 us
  local copies, waits for them, and re-layouts  68.4 us (45%)
  matrix products  33.9 us (22%)
  other arithmetic  25.2 us (16%)
  between operations  13.5 us (9%)
  starting transfers between devices  8.57 us (6%)
  loops' own time  2.32 us (2%)
    reshape x1, local copies, waits for them, and re-layouts, long_conv(): jnp.tile(pattern, (1, block))[:, :block * span]  29.6 us
    dot_general x4, matrix products, one_block(): jnp.einsum('gts,sgc->tgc', toeplitz, window, preferred_element_type=jnp.f...  24.5 us
    unnamed x5, local copies, waits for them, and re-layouts  12.7 us
    dot_general x1, matrix products, on_device(): jnp.dot(gated, lax.all_gather(out_weight, 'ctx', axis=1, tiled=True), pre...  9.39 us
    ppermute x2, starting transfers between devices, shifted(): return lax.ppermute(block, axis, route)  8.57 us
    convert_element_type x1, other arithmetic, on_device(): (gate_rows * (conv + conv_bias * carried.astype(jnp.float32))).astype(jnp...  7.81 us
    slice x1, local copies, waits for them, and re-layouts, long_conv(): jnp.tile(pattern, (1, block))[:, :block * span]  7.45 us
    add x1, other arithmetic, short_mixed(): return total + short_filter[2] * source[0:row_count]  6.62 us
  transfers between devices with their start and end apart: 3, of which 0 were waited for; matrix products, arithmetic and copies ran while one was open for 77% of the time, Pallas kernels for 0%

commit v1 on v0

v1 whole, which is shorter than its diff:
```python
import functools

import jax
import jax.numpy as jnp
from jax import lax
from jax.experimental import pallas as pl
from jax.experimental.pallas import tpu as pltpu
from jax.sharding import PartitionSpec as P

F32 = jnp.float32
BF16 = jnp.bfloat16
MESH = pl.DeviceIdType.MESH
LANES = 128
CHUNK = 256
EDGE = 16
SIDE = 608


def layer_kernel(
    tok, proj, sf, lf, cb, w, out,
    pv, xv, xr, tv, hr, wv, gv, tk, ob,
    ring_s, ring_r, x_s, x_r, sib_s, sib_r, halo_s, halo_r, loc, out_s,
):
    rows, channels = tok.shape[0], w.shape[0]
    taps = lf.shape[1]
    chunks = channels // CHUNK
    middle = channels - 2 * SIDE
    shard = w.shape[1]

    grp = lax.axis_index("groups")
    me = lax.axis_index("ctx")
    devices = lax.axis_size("ctx")
    core = me % 2
    chip = me // 2
    ring = devices // 2
    depth = ring // 2
    cz, cy = chip // 2, chip % 2
    pos = cz * (1 - cy) + (ring - 1 - cz) * cy

    def chip_at(position):
        q = (position + ring) % ring
        qy = q // depth
        qz = q * (1 - qy) + (ring - 1 - q) * qy
        return qz * 2 + qy

    def device_at(position):
        return chip_at(position) * 2 + core

    right = (grp, device_at(pos + 1))
    left = (grp, device_at(pos - 1))
    across = (1 - grp, me)
    sibling = (grp, me + 1 - 2 * core)
    following = (grp, (me + 1) % devices)
    previous = (grp, (me + devices - 1) % devices)
    has_next = me < devices - 1
    has_prev = me > 0

    tail = taps + EDGE
    head = rows - tail
    load_tail = pltpu.make_async_copy(proj.at[pl.ds(head, tail)], pv.at[pl.ds(EDGE + head, tail)], loc.at[0])
    load_head = pltpu.make_async_copy(proj.at[pl.ds(0, head)], pv.at[pl.ds(EDGE, head)], loc.at[1])
    load_tok = pltpu.make_async_copy(tok, tk, loc.at[2])
    load_w = pltpu.make_async_copy(w, wv.at[me], loc.at[3])
    load_tail.start()
    load_head.start()
    load_w.start()
    load_tok.start()

    barrier = pltpu.get_barrier_semaphore()
    for other in (left, right, across, sibling, following, previous):
        pl.semaphore_signal(barrier, inc=1, device_id=other, device_id_type=MESH)
    pl.semaphore_wait(barrier, 6)

    def remote(src, dst, ssem, rsem, dev):
        return pltpu.make_async_remote_copy(
            src_ref=src, dst_ref=dst, send_sem=ssem, recv_sem=rsem, device_id=dev, device_id_type=MESH
        )

    def span(step, d, piece):
        size = middle if piece == 1 else SIDE
        if piece == 0:
            start = grp * (SIDE + middle)
        elif piece == 1:
            start = SIDE
        else:
            start = (1 - grp) * (SIDE + middle)
        if step == depth:
            size = size // 2
            start = start + d * size
        return pl.ds(pl.multiple_of(start, EDGE), size)

    def owner(step, d):
        return device_at(pos - step) if d == 0 else device_at(pos + step)

    def ring_copy(step, d, piece):
        own = owner(step - 1, d)
        sp = span(step, d, piece)
        i = (step - 1) * 4 + d * 2 + piece
        src = w.at[sp] if step == 1 else wv.at[own, sp]
        return remote(src, wv.at[own, sp], ring_s.at[i], ring_r.at[i], right if d == 0 else left)

    def across_copy(step, d, piece=0):
        own = owner(step, d)
        sp = span(step, d, piece)
        i = (step - 1) * 2 + d
        return remote(wv.at[own, sp], wv.at[own, sp], x_s.at[i], x_r.at[i], across)

    def sibling_copy(step, d, piece):
        own = owner(step, d)
        sp = span(step, d, piece)
        i = (step - 1) * 6 + d * 3 + piece
        return remote(wv.at[own, sp], wv.at[own, sp], sib_s.at[i], sib_r.at[i], sibling)

    own_sib = remote(w, wv.at[me], sib_s.at[depth * 6], sib_r.at[depth * 6], sibling)
    edge_copy = remote(
        proj.at[pl.ds(rows - EDGE, EDGE)], pv.at[pl.ds(0, EDGE)], halo_s.at[0], halo_r.at[0], following
    )
    halo_copy = remote(
        xv.at[pl.ds(rows, taps)], xv.at[pl.ds(0, taps)], halo_s.at[1], halo_r.at[1], following
    )

    def ring_arrival(step, d, piece):
        own = owner(step, d)
        sp = span(step, d, piece)
        i = (step - 1) * 4 + d * 2 + piece
        remote(wv.at[own, sp], wv.at[own, sp], ring_s.at[i], ring_r.at[i], right).wait_recv()
        if step < depth:
            ring_copy(step + 1, d, piece).start()
        if piece == 0:
            across_copy(step, d).start()
        sibling_copy(step, d, piece).start()

    def across_arrival(step, d):
        across_copy(step, d, 2).wait_recv()
        sibling_copy(step, d, 2).start()

    @pl.when(has_next)
    def _():
        edge_copy.start()

    for piece in (0, 1):
        for d in (0, 1):
            ring_copy(1, d, piece).start()
    own_sib.start()

    def ring_both(step, piece):
        ring_arrival(step, 0, piece)
        ring_arrival(step, 1, piece)

    def across_both(step):
        across_arrival(step, 0)
        across_arrival(step, 1)

    def at(index, k, *events):
        @pl.when(k == index)
        def _():
            for fn, *args in events:
                fn(*args)

    def mix(r0, count, c0, width):
        cols = pl.ds(pl.multiple_of(c0, LANES), width)
        x = pv[pl.ds(pl.multiple_of(r0, EDGE), count + EDGE), cols].astype(F32)
        total = sf[0:1, cols] * x[EDGE:]
        total = total + sf[1:2, cols] * x[EDGE - 1 : -1]
        return total + sf[2:3, cols] * x[EDGE - 2 : -2]

    strip = 64

    def carry_strip(r0, c0):
        prod = mix(r0, strip, channels + c0, LANES) * mix(r0, strip, 2 * channels + c0, LANES)
        at_rows = pl.ds(pl.multiple_of(taps + r0, EDGE), strip)
        cols = pl.ds(pl.multiple_of(c0, LANES), LANES)
        xv[at_rows, cols] = prod.astype(BF16)
        xr[at_rows, cols] = pltpu.roll(prod, LANES // 2, 1).astype(BF16)

    load_tail.wait()
    tiles = channels // LANES

    @pl.loop(0, tiles)
    def _(t):
        for r in range(rows - taps, rows, strip):
            carry_strip(r, t * LANES)

    @pl.when(has_next)
    def _():
        halo_copy.start()

    jj = lax.broadcasted_iota(jnp.int32, (taps, 2 * taps), 0)
    ss = lax.broadcasted_iota(jnp.int32, (taps, 2 * taps), 1)
    flip = jnp.where(ss == taps - jj, 1.0, 0.0).astype(BF16)
    hr[...] = jnp.dot(lf[...], flip, preferred_element_type=F32)

    @pl.when(me == 0)
    def _():
        pv[0:EDGE, :] = jnp.zeros((EDGE, pv.shape[1]), BF16)
        xv[0:taps, :] = jnp.zeros((taps, channels), BF16)

    @pl.when(has_prev)
    def _():
        edge_copy.wait_recv()

    load_head.wait()

    def build_taps(g):
        row = jnp.broadcast_to(hr[pl.ds(g, 1), :], (taps, 2 * taps))
        mat = pltpu.roll(row, 0, 1, stride=1, stride_axis=0)
        tv[pl.ds(pl.multiple_of(g * taps, taps), taps), :] = mat.astype(BF16)

    per_tile = lf.shape[0] // tiles

    @pl.loop(0, tiles)
    def _(t):
        for r in range(0, rows - taps, strip):
            carry_strip(r, t * LANES)

        @pl.loop(0, per_tile)
        def _(i):
            build_taps(t * per_tile + i)

        at(7, t, (ring_both, 1, 0))
        at(13, t, (ring_both, 1, 1))

    @pl.when(has_prev)
    def _():
        halo_copy.wait_recv()

    half = LANES // 2
    quarter = per_tile // 2
    gw = half // quarter
    pairs = rows // (2 * taps)
    low = lax.broadcasted_iota(jnp.int32, (1, LANES), 1) < half

    def conv_tile(t):
        c0 = t * LANES
        cols = pl.ds(pl.multiple_of(c0, LANES), LANES)
        lows, highs = [], []
        for j in range(pairs):
            a = xv[pl.ds(j * 2 * taps, 2 * taps), cols]
            b = xr[pl.ds(j * 2 * taps + taps, 2 * taps), cols]
            lows.append(jnp.where(low, a, b))
            highs.append(jnp.where(low, b, a))
        parts = []
        lane = lax.broadcasted_iota(jnp.int32, (1, pairs * LANES), 1)
        which = (lane % half) // gw
        for side, blocks in enumerate((lows, highs)):
            rhs = jnp.concatenate(blocks, axis=1)
            first = (t * per_tile + side * quarter) * taps
            res = jnp.dot(
                tv[pl.ds(pl.multiple_of(first, taps), quarter * taps), :], rhs, preferred_element_type=F32
            )
            total = res[0:taps]
            for i in range(1, quarter):
                total = jnp.where(which == i, res[i * taps : (i + 1) * taps], total)
            parts.append(total)
        for j in range(pairs):
            z1 = parts[0][:, j * LANES : (j + 1) * LANES]
            z2 = parts[1][:, j * LANES : (j + 1) * LANES]
            even = jnp.where(low, z1, z2)
            odd = pltpu.roll(jnp.where(low, z2, z1), half, 1)
            for b, conv in ((2 * j, even), (2 * j + 1, odd)):
                r0 = b * taps
                carried = xv[pl.ds(taps + r0, taps), cols].astype(F32)
                gate = mix(r0, taps, c0, LANES)
                gv[pl.ds(r0, taps), cols] = (gate * (conv + cb[0:1, cols] * carried)).astype(BF16)

    @pl.loop(0, tiles)
    def _(t):
        conv_tile(t)
        at(1, t, (across_both, 1))
        at(4, t, (ring_both, 2, 0))
        at(8, t, (ring_both, 2, 1))
        at(11, t, (across_both, 2))
        at(14, t, (ring_both, 3, 0))

    load_tok.wait()
    load_w.wait()

    def sibling_wait(step, d):
        for piece in range(3):
            sibling_copy(step, d, piece).wait_recv()

    blocks = ring
    width = 2 * shard

    def out_copy(idx):
        sign = 1 - 2 * (idx % 2)
        c = chip_at(pos + ((idx + 1) // 2) * sign)
        cols = pl.ds(pl.multiple_of(c * width, width), width)
        return pltpu.make_async_copy(ob.at[:, cols], out.at[:, cols], out_s.at[idx])

    @pl.loop(0, blocks)
    def _(idx):
        at(0, idx, (own_sib.wait_recv,))
        at(1, idx, (sibling_wait, 1, 0))
        at(2, idx, (sibling_wait, 1, 1), (ring_both, 3, 1))
        at(3, idx, (sibling_wait, 2, 0))
        at(4, idx, (sibling_wait, 2, 1), (across_both, 3), (ring_both, 4, 0), (ring_both, 4, 1))
        at(5, idx, (sibling_wait, 3, 0))
        at(6, idx, (sibling_wait, 3, 1), (across_both, 4))
        at(7, idx, (sibling_wait, depth, 0), (sibling_wait, depth, 1))
        sign = 1 - 2 * (idx % 2)
        c = chip_at(pos + ((idx + 1) // 2) * sign)
        cols = pl.ds(pl.multiple_of(c * width, width), width)

        rhs = jnp.concatenate([wv[2 * c], wv[2 * c + 1]], axis=1)
        branch = jnp.dot(gv[...], rhs, preferred_element_type=F32)
        ob[:, cols] = (tk[:, cols].astype(F32) + branch).astype(BF16)
        out_copy(idx).start()

    for step in range(1, depth + 1):
        for d in (0, 1):
            ring_copy(step, d, 0).wait_send()
            ring_copy(step, d, 1).wait_send()
            across_copy(step, d).wait_send()
            for piece in range(3):
                sibling_copy(step, d, piece).wait_send()
    own_sib.wait_send()

    @pl.when(has_next)
    def _():
        edge_copy.wait_send()
        halo_copy.wait_send()

    for idx in range(blocks):
        out_copy(idx).wait()


def on_device(tokens, projected, short_filter, long_filter, conv_bias, out_weight):
    rows, channels = tokens.shape[0], out_weight.shape[0]
    taps = long_filter.shape[1]
    devices = lax.axis_size("ctx")
    chips = devices // 2
    depth = chips // 2
    anyspace = pl.BlockSpec(memory_space=pl.ANY)
    vmem = pl.BlockSpec(memory_space=pltpu.VMEM)
    dma = pltpu.SemaphoreType.DMA
    return pl.pallas_call(
        layer_kernel,
        out_shape=jax.ShapeDtypeStruct(tokens.shape, BF16),
        in_specs=[anyspace, anyspace, vmem, vmem, vmem, anyspace],
        out_specs=anyspace,
        scratch_shapes=[
            pltpu.VMEM((rows + EDGE, projected.shape[1]), BF16),
            pltpu.VMEM((rows + taps, channels), BF16),
            pltpu.VMEM((rows + taps, channels), BF16),
            pltpu.VMEM((long_filter.shape[0] * taps, 2 * taps), BF16),
            pltpu.VMEM((long_filter.shape[0], 2 * taps), F32),
            pltpu.VMEM((devices, channels, out_weight.shape[1]), BF16),
            pltpu.VMEM((rows, channels), BF16),
            pltpu.VMEM(tokens.shape, BF16),
            pltpu.VMEM(tokens.shape, BF16),
            dma((depth * 4,)),
            dma((depth * 4,)),
            dma((depth * 2,)),
            dma((depth * 2,)),
            dma((depth * 6 + 1,)),
            dma((depth * 6 + 1,)),
            dma((2,)),
            dma((2,)),
            dma((4,)),
            dma((chips,)),
        ],
        compiler_params=pltpu.CompilerParams(
            collective_id=0, has_side_effects=True, vmem_limit_bytes=52 * 1024 * 1024
        ),
        cost_estimate=pl.CostEstimate(flops=2 * rows * channels * channels, bytes_accessed=20_000_000, transcendentals=0),
    )(tokens, projected, short_filter, long_filter, conv_bias.reshape(1, -1), out_weight)


def shifted(block, axis, distance):
    devices = range(lax.axis_size(axis))
    route = [(i - distance, i) for i in devices if i - distance in devices]
    return lax.ppermute(block, axis, route)


def general(tokens, projected, short_filter, long_filter, conv_bias, out_weight):
    rows, channels = tokens.shape[0], out_weight.shape[0]
    groups, taps = long_filter.shape
    edge = shifted(projected[rows - 2 :], "ctx", 1)
    source = jnp.concatenate([edge, projected], axis=0).astype(F32)
    mixed = short_filter[0] * source[2:] + short_filter[1] * source[1:-1] + short_filter[2] * source[:-2]
    carried = (mixed[:, channels : 2 * channels] * mixed[:, 2 * channels :]).astype(BF16)
    extended = jnp.concatenate([shifted(carried[rows - taps + 1 :], "ctx", 1), carried], axis=0)
    block = min(128, rows)
    width = block + taps - 1
    pattern = jnp.concatenate([long_filter[:, ::-1], jnp.zeros((groups, block), BF16)], axis=1)
    toeplitz = jnp.tile(pattern, (1, block))[:, : block * width].reshape(groups, block, width)
    grouped = extended.reshape(extended.shape[0], groups, -1)

    def one_block(index):
        window = lax.dynamic_slice_in_dim(grouped, index * block, width, 0)
        return jnp.einsum("gts,sgc->tgc", toeplitz, window, preferred_element_type=F32).reshape(block, -1)

    conv = lax.map(one_block, jnp.arange(rows // block, dtype=jnp.int32)).reshape(rows, -1)
    gated = (mixed[:, :channels] * (conv + conv_bias * carried.astype(F32))).astype(BF16)
    whole = lax.all_gather(out_weight, "ctx", axis=1, tiled=True)
    branch = jnp.dot(gated, whole, preferred_element_type=F32)
    return (tokens.astype(F32) + branch).astype(BF16)


def solution(mesh):
    fits = mesh.shape["groups"] == 2 and mesh.shape["ctx"] == 16
    placed = (P(("groups", "ctx"), None), P(("groups", "ctx"), None), P(), P(), P(), P(None, "ctx"))
    return jax.shard_map(
        on_device if fits else general,
        mesh=mesh, in_specs=placed, out_specs=P(("groups", "ctx"), None), check_vma=False,
    )
```

time: 153 us -> 58.9 us (0.38)
  local copies, waits for them, and re-layouts: 68.4 us -> 6.55 us
  Pallas kernels: 0 us -> 52 us
  matrix products: 33.9 us -> 0 us
  other arithmetic: 25.2 us -> 0 us
  between operations: 13.5 us -> 0.01 us
  starting transfers between devices: 8.57 us -> 0 us
  loops' own time: 2.32 us -> 0 us
    pallas_call x0 -> x1, Pallas kernels: none -> 52 us  [on_device(): pl.pallas_call(layer_kernel, out_shape=jax.ShapeDtypeStruct(tokens.shape,...]
    dot_general x5 -> x0, matrix products: 33.9 us -> none  [the longest x4 24.5 us: one_block(): jnp.einsum('gts,sgc->tgc', toeplitz, window, preferred_element_type=jnp.f...]
    reshape x1 -> x0, local copies, waits for them, and re-layouts: 29.6 us -> none  [long_conv(): jnp.tile(pattern, (1, block))[:, :block * span]]
    convert_element_type x3 -> x0, other arithmetic: 16.6 us -> none  [the longest x1 7.81 us: on_device(): (gate_rows * (conv + conv_bias * carried.astype(jnp.float32))).astype(jnp...]
    slice x4 -> x0, local copies, waits for them, and re-layouts: 9.61 us -> none  [the longest x1 7.45 us: long_conv(): jnp.tile(pattern, (1, block))[:, :block * span]]
    ppermute x2 -> x0, starting transfers between devices: 8.57 us -> none  [shifted(): return lax.ppermute(block, axis, route)]
    add x1 -> x0, other arithmetic: 6.62 us -> none  [short_mixed(): return total + short_filter[2] * source[0:row_count]]
    unnamed x5 -> x9, local copies, waits for them, and re-layouts: 12.7 us -> 6.55 us
  transfers between devices with their start and end apart: 3 -> 0, of which waited for: 0 -> 0; matrix products, arithmetic and copies ran while one was open for 77% -> 0% of each run, Pallas kernels for 0% -> 0%
where the time goes in v1:
time: 58.9 us; the launch traced here: 58.5 us
  Pallas kernels  52 us (88%)
  local copies, waits for them, and re-layouts  6.55 us (11%)
    pallas_call x1, Pallas kernels, on_device(): pl.pallas_call(layer_kernel, out_shape=jax.ShapeDtypeStruct(tokens.shape,...  52 us
    unnamed x9, local copies, waits for them, and re-layouts  6.55 us

profile of v1, /device:TPU:1, one launch (start us, length us, event | category | flops | bytes accessed | tf_op | source)
XLA Modules:
  0.0 58.5 jit_solution(11070930461555459325)
XLA Ops:
  0.0 0.0 copy-start
  0.0 1.0 %copy-done = bf16[2048,128]{1,0:T(8,128)(2,1)S(1)} copy-done((bf16[2048,128]{1,0:T(8,128)(2,1)S(1)}, bf16[2048,128]{1,0:T(8,128)(2,1)}, u32[]{:S(2)}) %copy-start) | copy-done | bytes 524312
  1.0 0.0 copy-start.1
  1.0 0.9 %copy-done.1 = f32[3,6144]{1,0:T(4,128)S(1)} copy-done((f32[3,6144]{1,0:T(4,128)S(1)}, f32[3,6144]{1,0:T(4,128)}, u32[]{:S(2)}) %copy-start.1) | copy-done | bytes 73752
  1.9 0.0 copy-start.2
  1.9 0.8 %copy-done.2 = bf16[128,128]{1,0:T(8,128)(2,1)S(1)} copy-done((bf16[128,128]{1,0:T(8,128)(2,1)S(1)}, bf16[128,128]{1,0:T(8,128)(2,1)}, u32[]{:S(2)}) %copy-start.2) | copy-done | bytes 32792
  2.7 0.0 copy-start.3
  2.7 0.7 %copy-done.3 = f32[2048]{0:T(1024)S(1)} copy-done((f32[2048]{0:T(1024)S(1)}, f32[2048]{0:T(1024)}, u32[]{:S(2)}) %copy-start.3) | copy-done | bytes 8216
  3.4 52.0 %shard_map.64 = bf16[512,2048]{1,0:T(8,128)(2,1)} custom-call(bf16[512,2048]{1,0:T(8,128)(2,1)} %tok.1, bf16[512,6144]{1,0:T(8,128)(2,1)} %proj.1, f32[3,6144]{1,0:T(4,128)S(1)} %copy-done.1, bf16[128,128]{1,0:T(8,128)(2,1)S(1)} %copy-done.2, f32[1,2048]{1,0:T(1,128)S(1)} %bitcast.1, bf16[2048,128]{1,0:T(8,128)(2,1)S(1)} %copy-done), custom_call_target="tpu_custom_call" | custom-call | flops 4294967296 | bytes 20000000 | tf_op jit(solution)/shard_map/pallas_call | solution.py:337
  55.4 3.2 %copy.8 = bf16[512,2048]{1,0:T(8,128)(2,1)} copy(bf16[512,2048]{1,0:T(8,128)(2,1)} %shard_map.64) | data formatting | bytes 4194304
Async XLA Ops:
  0.0 1.0 %copy-start = (bf16[2048,128]{1,0:T(8,128)(2,1)S(1)}, bf16[2048,128]{1,0:T(8,128)(2,1)}, u32[]{:S(2)}) copy-start(bf16[2048,128]{1,0:T(8,128)(2,1)} %w.1) | copy-start | bytes 1572868
  1.0 0.9 %copy-start.1 = (f32[3,6144]{1,0:T(4,128)S(1)}, f32[3,6144]{1,0:T(4,128)}, u32[]{:S(2)}) copy-start(f32[3,6144]{1,0:T(4,128)} %sf.1) | copy-start | bytes 221188
  1.9 0.8 %copy-start.2 = (bf16[128,128]{1,0:T(8,128)(2,1)S(1)}, bf16[128,128]{1,0:T(8,128)(2,1)}, u32[]{:S(2)}) copy-start(bf16[128,128]{1,0:T(8,128)(2,1)} %lf.1) | copy-start | bytes 98308
  2.7 0.7 %copy-start.3 = (f32[2048]{0:T(1024)S(1)}, f32[2048]{0:T(1024)}, u32[]{:S(2)}) copy-start(f32[2048]{0:T(1024)} %param.10) | copy-start | bytes 24580

commit v2 on v1

--- a/solution.py
+++ b/solution.py
@@ -17,8 +17,8 @@
 
 
 def layer_kernel(
-    tok, proj, sf, lf, cb, w, out,
-    pv, xv, xr, tv, hr, wv, gv, tk, ob,
+    tok, proj, sf_in, lf_in, cb_in, w, out,
+    pv, xv, xr, tv, hr, wv, gv, tk, ob, sf, lf, cb,
     ring_s, ring_r, x_s, x_r, sib_s, sib_r, halo_s, halo_r, loc, out_s,
 ):
     rows, channels = tok.shape[0], w.shape[0]
@@ -61,7 +61,13 @@
     load_head = pltpu.make_async_copy(proj.at[pl.ds(0, head)], pv.at[pl.ds(EDGE, head)], loc.at[1])
     load_tok = pltpu.make_async_copy(tok, tk, loc.at[2])
     load_w = pltpu.make_async_copy(w, wv.at[me], loc.at[3])
+    load_sf = pltpu.make_async_copy(sf_in, sf, loc.at[4])
+    load_lf = pltpu.make_async_copy(lf_in, lf, loc.at[5])
+    load_cb = pltpu.make_async_copy(cb_in, cb, loc.at[6])
+    load_sf.start()
+    load_lf.start()
     load_tail.start()
+    load_cb.start()
     load_head.start()
     load_w.start()
     load_tok.start()
@@ -173,6 +179,9 @@
         xv[at_rows, cols] = prod.astype(BF16)
         xr[at_rows, cols] = pltpu.roll(prod, LANES // 2, 1).astype(BF16)
 
+    load_sf.wait()
+    load_lf.wait()
+    load_cb.wait()
     load_tail.wait()
     tiles = channels // LANES
 
@@ -332,12 +341,11 @@
     chips = devices // 2
     depth = chips // 2
     anyspace = pl.BlockSpec(memory_space=pl.ANY)
-    vmem = pl.BlockSpec(memory_space=pltpu.VMEM)
     dma = pltpu.SemaphoreType.DMA
     return pl.pallas_call(
         layer_kernel,
         out_shape=jax.ShapeDtypeStruct(tokens.shape, BF16),
-        in_specs=[anyspace, anyspace, vmem, vmem, vmem, anyspace],
+        in_specs=[anyspace] * 6,
         out_specs=anyspace,
         scratch_shapes=[
             pltpu.VMEM((rows + EDGE, projected.shape[1]), BF16),
@@ -349,6 +357,9 @@
             pltpu.VMEM((rows, channels), BF16),
             pltpu.VMEM(tokens.shape, BF16),
             pltpu.VMEM(tokens.shape, BF16),
+            pltpu.VMEM(short_filter.shape, F32),
+            pltpu.VMEM(long_filter.shape, BF16),
+            pltpu.VMEM((1, channels), F32),
             dma((depth * 4,)),
             dma((depth * 4,)),
             dma((depth * 2,)),
@@ -357,11 +368,11 @@
             dma((depth * 6 + 1,)),
             dma((2,)),
             dma((2,)),
-            dma((4,)),
+            dma((7,)),
             dma((chips,)),
         ],
         compiler_params=pltpu.CompilerParams(
-            collective_id=0, has_side_effects=True, vmem_limit_bytes=52 * 1024 * 1024
+            collective_id=0, has_side_effects=True, vmem_limit_bytes=63 * 1024 * 1024
         ),
         cost_estimate=pl.CostEstimate(flops=2 * rows * channels * channels, bytes_accessed=20_000_000, transcendentals=0),
     )(tokens, projected, short_filter, long_filter, conv_bias.reshape(1, -1), out_weight)

time: 58.9 us -> 55 us (0.934)
  local copies, waits for them, and re-layouts: 6.55 us -> 3.16 us
    unnamed x9 -> x1, local copies, waits for them, and re-layouts: 6.55 us -> 3.16 us
where the time goes in v2:
time: 55 us; the launch traced here: 54.8 us
  Pallas kernels  51.7 us (94%)
  local copies, waits for them, and re-layouts  3.16 us (6%)
    pallas_call x1, Pallas kernels, on_device(): pl.pallas_call(layer_kernel, out_shape=jax.ShapeDtypeStruct(tokens.shape,...  51.7 us
    unnamed x1, local copies, waits for them, and re-layouts  3.16 us

profile of v2, /device:TPU:1, one launch (start us, length us, event | category | flops | bytes accessed | tf_op | source)
XLA Modules:
  0.0 54.8 jit_solution(5920345886841762746)
XLA Ops:
  0.0 51.7 %shard_map.64 = bf16[512,2048]{1,0:T(8,128)(2,1)} custom-call(bf16[512,2048]{1,0:T(8,128)(2,1)} %tok.1, bf16[512,6144]{1,0:T(8,128)(2,1)} %proj.1, f32[3,6144]{1,0:T(4,128)} %sf_in.1, bf16[128,128]{1,0:T(8,128)(2,1)} %lf_in.1, f32[1,2048]{1,0:T(1,128)} %bitcast.1, bf16[2048,128]{1,0:T(8,128)(2,1)} %w.1), custom_call_target="tpu_custom_call" | custom-call | flops 4294967296 | bytes 20000000 | tf_op jit(solution)/shard_map/pallas_call | solution.py:345
  51.7 3.2 %copy.8 = bf16[512,2048]{1,0:T(8,128)(2,1)} copy(bf16[512,2048]{1,0:T(8,128)(2,1)} %shard_map.64) | data formatting | bytes 4194304
